TPU v7x, 32 devices: a whole 2x2x4 slice. The times are simulated.
32 devices in a mesh: seq: 4 (over y, x), batch: 8 (over z, core).
Axes of the slice: x: 2, y: 2, z: 4, core: 2. Of those that a mesh axis runs over, the one named last changes fastest.
Arguments:
- inputs: bfloat16 [8, 2048, 768], P('batch', 'seq'), may hold values from -6 to 6
- doc_ids: int32 [8, 2048], P('batch'), may hold values from 0 to 6, as said below
- w_qkv: bfloat16 [768, 896], replicated, may hold values from -0.3125 to 0.3125
- b_qkv: float32 [896], replicated, may hold values from -3 to 3
- w_o: bfloat16 [768, 768], replicated, may hold values from -0.875 to 0.875
- w_fc: bfloat16 [768, 3072], replicated, may hold values from -0.21875 to 0.21875
- b_fc: float32 [3072], replicated, may hold values from -3 to 3
- w_proj: bfloat16 [3072, 768], replicated, may hold values from -0.109375 to 0.109375
- b_proj: float32 [768], replicated, may hold values from -3 to 3
- gain_one: float32 [768], replicated, may hold values from 0.1 to 1.9
- shift_one: float32 [768], replicated, may hold values from -1.75 to 1.75
- gain_two: float32 [768], replicated, may hold values from 0.1 to 1.9
- shift_two: float32 [768], replicated, may hold values from -1.75 to 1.75
- cotangent: bfloat16 [8, 2048, 768], P('batch', 'seq'), may hold values from -6 to 6
Outputs:
- outputs: bfloat16 [8, 2048, 768], P('batch', 'seq')
- input_grads: bfloat16 [8, 2048, 768], P('batch', 'seq')
- grad_w_qkv: float32 [768, 896], P('batch')
- grad_b_qkv: float32 [896], P('batch')
- grad_w_o: float32 [768, 768], P('batch')
- grad_w_fc: float32 [768, 3072], P('batch')
- grad_b_fc: float32 [3072], P('batch')
- grad_w_proj: float32 [3072, 768], P('batch')
- grad_b_proj: float32 [768], P('batch')
- grad_gain_one: float32 [768], P('batch')
- grad_shift_one: float32 [768], P('batch')
- grad_gain_two: float32 [768], P('batch')
- grad_shift_two: float32 [768], P('batch')
Inputs may be any that keep to these rules, and one draw needn't show every extreme that they name: `doc_ids`: along each row the ids never fall; in every row one document begins within the first 512 positions and ends within the last 512.
All inputs are finite; a program needn't handle non-finite values.
Results may differ from a plain program's by a relative error of at most 0.017.
Values may be sent and summed in bfloat16 or wider, within the bound.
A program may use at most 320 MiB of HBM per device.

v0:
```python
import functools
import math
import types

import jax
import jax.numpy as jnp
import numpy as np
from jax import lax
from jax.experimental import pallas as pl
from jax.experimental.pallas import tpu as pltpu
from jax.sharding import PartitionSpec as P

HEAD = 64
ROT = 16
EPSILON = 1e-05
LANES = 128
BLOCK = 256
FAR = -1e30
LOG2E = math.log2(math.e)
MESH = pl.DeviceIdType.MESH
F32 = jnp.float32
BF16 = jnp.bfloat16

PIECE = 96
SLOTS = 4


class Chunk:
    def __init__(self, name, kind, height, count, base, lane):
        self.name, self.kind = name, kind
        self.height, self.count, self.base, self.lane = height, count, base, lane

    @property
    def rows(self):
        return self.height * self.count * (2 if self.kind == "whole" else 8)

    def place(self, core, p, s, i):
        if self.kind == "whole":
            at = core * 4 + i
        elif self.kind == "line":
            at = ((core * 4 + i) * 2 + p) * 2 + s
        else:
            at = ((core * 2 + p) * 2 + s) * self.count + i
        return self.base + at * self.height

    def ref(self, r):
        if self.lane is None:
            return r.grads
        return r.wp.at[:, self.lane * BLOCK : (self.lane + 1) * BLOCK]

    @staticmethod
    def split(core, y, x):
        return (y, x) if core else (x, y)

    def unfold(self, array):
        array = array[self.base : self.base + self.rows]
        if self.kind == "whole":
            return array.reshape(2, 4, self.height, BLOCK)
        if self.kind == "line":
            array = array.reshape(2, 4, 2, 2, self.height, BLOCK).transpose(0, 2, 3, 1, 4, 5)
        else:
            array = array.reshape(2, 2, 2, self.count, self.height, BLOCK)
        return jnp.stack([array[0].swapaxes(0, 1), array[1]])


def make_chunks():
    plans = [
        ("p0", "plane", PIECE, 3, None),
        ("p1", "plane", PIECE, 3, None),
        ("f0", "line", PIECE, 4, None),
        ("p2", "plane", PIECE, 3, None),
        ("f1", "block", PIECE, 4, None),
        ("p3", "plane", PIECE, 3, None),
        ("f2", "block", PIECE, 4, None),
        ("uc", "block", PIECE // 2, 4, 1),
        ("ua", "block", PIECE // 2, 4, 0),
        ("ub", "block", PIECE // 2, 4, 0),
        ("k", "whole", PIECE // 2, 4, 1),
        ("v", "whole", 16, 4, 1),
    ]
    chunks, filled = {}, {}
    for name, kind, height, count, lane in sorted(plans, key=lambda plan: plan[1] != "plane"):
        chunk = Chunk(name, kind, height, count, filled.get(lane, 0), lane)
        chunks[name] = chunk
        filled[lane] = chunk.base + chunk.rows
    return {plan[0]: chunks[plan[0]] for plan in plans}, filled[None]


CHUNKS, GRAD_ROWS = make_chunks()


def mm(a, b, ca=1, cb=0):
    return lax.dot_general(a, b, (((ca,), (cb,)), ((), ())), preferred_element_type=F32)


def flip(value):
    return value.astype(F32).T


def lanes_of(shape):
    return lax.broadcasted_iota(jnp.int32, shape, 1)


def rows_of(shape):
    return lax.broadcasted_iota(jnp.int32, shape, 0)


EARLY_DONE = 64

FEED_SCHEDULE = [
    ([], ["send:p0"], []),
    (["a:p0"], [], ["send:p1", "send:f0"]),
    (["a:f0", "a:p1"], ["send:p2"], ["send:f1"]),
    (["b:p0"], ["a:f1", "send:p3"], []),
    [],
]

SCHEDULE = {
    4: ["a:p2", "send:f2"],
    12: ["c:p0", "a:f2"],
    16: ["b:f1"],
    20: ["a:p3"],
    28: ["b:f2"],
    32: ["c:f1"],
    36: ["b:f0", "b:p2"],
    44: ["c:f2", "b:p1"],
    48: ["c:f0"],
    60: ["b:p3", "d:f1"],
    EARLY_DONE: ["make:uc", "d:f2", "send:uc", "c:p1"],
    68: ["c:p2", "a:uc"],
    72: ["g:f2", "c:p3", "g:f1"],
    76: ["b:uc", "d:f0"],
}

LATE_SCHEDULE = [
    [],
    ["send:ua", "c:uc", "e:f1", "a:ua", "e:f2", "send:ub", "a:ub"],
    ["send:k", "b:ua", "g:f0", "a:k"],
    ["b:ub", "send:v", "d_planes:p0", "c:ua", "d:uc", "a:v", "c:ub", "d:k", "e:f0", "g:p0", "d:ua", "d:v", "d:ub"],
    ["e:uc", "e:v", "e:ua", "e:p0", "e:ub", "e:k"],
]

LENT = 5


def gelu_parts(hidden):
    size = jnp.abs(hidden)
    t = pl.reciprocal(1.0 + (0.3275911 / math.sqrt(2.0)) * size)
    bell = jnp.exp2(hidden * hidden * (-0.5 * LOG2E))
    poly = 0.5 * 1.061405429
    for term in (-1.453152027, 1.421413741, -0.284496736, 0.254829592):
        poly = poly * t + 0.5 * term
    tail = poly * t * bell
    below = jnp.where(hidden >= 0, 1.0 - tail, tail)
    return below, hidden * bell * (1.0 / math.sqrt(2.0 * math.pi))


def layer_kernel(names, parts, inside, *refs):
    r = types.SimpleNamespace(**dict(zip(names, refs, strict=True)))
    span, width = r.x.shape
    hidden_units = r.wfc.shape[1]
    heads = width // HEAD
    mine = lax.axis_index("seq")
    batch = lax.axis_index("batch")
    partner = parts - 1 - mine
    high = jnp.maximum(mine, partner)

    loads = [
        pltpu.make_async_copy(src, dst, r.load_sem.at[i])
        for i, (src, dst) in enumerate(
            [(r.x_h, r.x), (r.wq_h, r.wq), (r.cot_h, r.cot), (r.wo_h, r.wo), (r.wfc_h, r.wfc), (r.wp_h, r.wp)]
        )
    ]
    for load in loads:
        load.start()

    barrier = pltpu.get_barrier_semaphore()
    peers = [(lax.rem(mine + distance, parts), batch) for distance in range(1, parts)]
    summing = Summing(r, mine, batch, parts) if inside else None
    if inside:
        peers += [summing.core_peer, *summing.z_peers]
    for peer in peers:
        pl.semaphore_signal(barrier, inc=1, device_id=peer, device_id_type=MESH)
    pl.semaphore_wait(barrier, len(peers))

    def keep(name, core, y, x, i, value):
        chunk = CHUNKS[name]
        row = chunk.place(core, *chunk.split(core, y, x), i)
        chunk.ref(r)[row : row + chunk.height, :] = value.astype(BF16)

    def step(steps):
        for item in steps if inside else ():
            kind, name = item.split(":")
            if kind == "make":
                make_early()
            else:
                getattr(summing, kind)(CHUNKS[name])

    loads[0].wait()

    def norm_tile(i):
        tokens = r.x[pl.ds(i * LANES, LANES), :].astype(F32)
        average = jnp.mean(tokens, axis=-1, keepdims=True)
        centered = tokens - average
        variance = jnp.mean(centered * centered, axis=-1, keepdims=True)
        inverse_std = lax.rsqrt(variance + EPSILON)
        return centered * inverse_std, inverse_std

    for i in range(span // LANES):
        normed, _ = norm_tile(i)
        rows = pl.ds(i * LANES, LANES)
        first = normed * r.g1[...][None] + r.s1[...][None]
        second = normed * r.g2[...][None] + r.s2[...][None]
        r.fi[rows, :] = first.astype(BF16)
        r.si[rows, :] = second.astype(BF16)
        r.fit[:, rows] = first.T.astype(BF16)
        r.sit[:, rows] = second.T.astype(BF16)

    half = ROT // 2
    index = rows_of((half, span))
    frequency = jnp.zeros((half, span), F32)
    for i in range(half):
        frequency = jnp.where(index == i, np.float32(10000.0 ** (-2.0 * i / ROT)), frequency)
    for i, part in enumerate((mine, partner)):
        angle = (part * span + lanes_of((half, span))).astype(F32) * frequency
        r.cos[i] = jnp.cos(angle)
        r.sin[i] = jnp.sin(angle)
    cosine, sine = r.cos[0], r.sin[0]
    ones = jnp.ones((HEAD - ROT, span), F32)
    zeros = jnp.zeros((HEAD - ROT, span), F32)
    table_cos = jnp.concatenate([cosine, cosine, ones] * 2, axis=0).T
    table_sin = jnp.concatenate([-sine, sine, zeros] * 2, axis=0).T
    lane = lanes_of((span, LANES))

    def rotate(tile, cos_of, sin_of):
        partner = jnp.where(
            lax.rem(lane, HEAD) < half, pltpu.roll(tile, LANES - half, 1), pltpu.roll(tile, half, 1)
        )
        return tile * cos_of + partner * sin_of

    def docs_row(part):
        return r.docs[0:1, pl.ds(pl.multiple_of(part * span, LANES), span)]

    loads[1].wait()
    key_value = mm(r.fi[...], r.wq[:, width:]) + r.bq[width:][None]
    low = lane < HEAD
    key_value = rotate(key_value, jnp.where(low, table_cos, 1.0), jnp.where(low, table_sin, 0.0))
    r.kv[mine] = key_value.astype(BF16)
    for distance in range(1, parts):
        kv_copy(r, mine, batch, parts, distance).start()

    feature_row = rows_of((LANES, span)) - HEAD

    def keep_queries(slot, tile, feature):
        for i, head in enumerate((tile, pltpu.roll(tile, HEAD, 1))):
            head = jnp.where(low, head, feature)
            r.q[slot + i] = head.astype(BF16)
            r.qt[slot + i] = head.T.astype(BF16)

    query_feature = jnp.where(feature_row == docs_row(mine), 1.0, 0.0).T
    for i in range(heads // 2):
        columns = slice(i * LANES, (i + 1) * LANES)
        tile = mm(r.fi[...], r.wq[:, columns]) + r.bq[columns][None]
        tile = rotate(tile, table_cos, table_sin) * (LOG2E / math.sqrt(HEAD))
        keep_queries(2 * i, tile, query_feature)
        if i == LENT:
            r.lent[...] = tile.astype(BF16)

    loads[2].wait()
    loads[3].wait()
    for i in range(width // BLOCK):
        rows = slice(i * BLOCK, (i + 1) * BLOCK)
        r.dot[rows, :] = mm(r.wo[rows, :], r.cot[...], 1, 1).astype(BF16)

    @pl.when(mine == parts - 1)
    def _():
        for copy in lent_copies(r, mine, batch, parts):
            copy.start()


    loads[4].wait()
    loads[5].wait()
    r.result[...] = jnp.zeros_like(r.result)
    r.second[...] = jnp.zeros_like(r.second)
    ones_rows = jnp.ones((8, span), BF16)
    group = 2 * 4 * 96

    def feed_steps(g, i):
        for group_of, steps in enumerate(FEED_SCHEDULE[:-1]):
            if steps[i]:

                @pl.when(g == group_of)
                def _():
                    step(steps[i])

    plane, line, block = CHUNKS["p0"], CHUNKS["f0"], CHUNKS["f1"]

    def feed_forward(g, _):
        columns = pl.ds(pl.multiple_of(g * group, LANES), group)
        hidden = mm(r.si[...], r.wfc[:, columns]) + r.bfc[columns][None]
        grad_act = mm(r.cot[...], r.wp[columns, :], 1, 1)
        below, slope = gelu_parts(hidden)
        r.act[...] = (hidden * below).astype(BF16)
        r.gh[...] = (grad_act * (below + slope)).astype(BF16)
        feed_steps(g, 0)
        grad_w = mm(r.act[...], r.cot[...], 0, 0)
        for c in range(2):
            for q in range(4):
                row = (c * 4 + q) * PIECE
                for k in range(3):
                    to = g * plane.rows + plane.place(c, *plane.split(c, q // 2, q % 2), k)
                    piece = grad_w[row : row + PIECE, k * BLOCK : (k + 1) * BLOCK]
                    r.grads[pl.ds(pl.multiple_of(to, 16), PIECE), :] = piece.astype(BF16)
        feed_steps(g, 1)
        grad_w = mm(r.sit[...], r.gh[...])
        for k in range(group // BLOCK):
            at = g * (group // BLOCK) + k
            chunk, y, x = at // 4, lax.rem(at, 4) // 2, lax.rem(at, 2)
            for b in range(8):
                c, z = b % 2, b // 2
                p, s = line.split(c, y, x)
                later = block.place(c, p, s, z) + (chunk - 1) * block.rows
                to = jnp.where(chunk == 0, line.place(c, p, s, z), later)
                piece = grad_w[b * PIECE : (b + 1) * PIECE, k * BLOCK : (k + 1) * BLOCK]
                r.grads[pl.ds(pl.multiple_of(to, 16), PIECE), :] = piece.astype(BF16)
        feed_steps(g, 2)
        r.sum_fc[:, columns] = mm(ones_rows, r.gh[...])
        r.result[...] += mm(r.act[...], r.wp[columns, :])
        r.second[...] += mm(r.gh[...], r.wfc[:, columns], 1, 1)
        return 0

    lax.fori_loop(0, hidden_units // group, feed_forward, 0)
    step(FEED_SCHEDULE[4])

    for distance in range(1, parts):
        kv_copy(r, lax.rem(mine - distance + parts, parts), batch, parts, distance).wait_recv()
    for part in range(parts):
        apart = (feature_row >= 0) & (feature_row < 8) & (feature_row != docs_row(part))
        key_feature = jnp.where(apart, FAR, 0.0).T
        pair = r.kv[part].astype(F32)
        keys = jnp.where(low, pair, key_feature)
        values = jnp.where(low, pltpu.roll(pair, HEAD, 1), jnp.where(lane < HEAD + 2, 1.0, 0.0))
        r.kx[part] = keys.astype(BF16)
        r.kxt[part] = keys.T.astype(BF16)
        r.vx[part] = values.astype(BF16)
        r.vxt[part] = values.T.astype(BF16)

    @pl.when(mine == 0)
    def _():
        for copy in lent_copies(r, mine, batch, parts):
            copy.wait_recv()
        feature = jnp.where(feature_row == docs_row(partner), 1.0, 0.0).T
        keep_queries(heads, r.lent_in[...].astype(F32), feature)

    r.dk[...] = jnp.zeros_like(r.dk)
    r.dv[...] = jnp.zeros_like(r.dv)

    def make_early():
        @pl.when(mine == parts - 1)
        def _():
            for copy in back_copies(r, mine, batch, parts):
                copy.wait_recv()

        grad_q = mm(r.fit[...], r.gqt[BLOCK:width, :], 1, 1)
        for b in range(8):
            for y in range(2):
                rows = slice(b * PIECE + y * PIECE // 2, b * PIECE + (y + 1) * PIECE // 2)
                for x in range(2):
                    keep("uc", b % 2, y, x, b // 2, grad_q[rows, x * BLOCK : (x + 1) * BLOCK])

    mid = span // 2

    def tiles_of(last):
        return [(part, 0, span, 0) for part in range(last)] + [(last, 0, mid, 0), (last, mid, mid, mid)]

    def spread(value, start):
        return jnp.concatenate([jnp.zeros((value.shape[0], start), F32), value], axis=1) if start else value

    def attend(slot, last):
        rows = pl.ds(pl.multiple_of(slot * HEAD, HEAD), HEAD)
        tiles = tiles_of(last)
        tops = []
        for part, k0, count, q0 in tiles:
            raw = mm(r.kx[part, k0 : k0 + count], r.qt[slot, :, q0:])
            if part == last:
                raw = jnp.where(rows_of(raw.shape) <= lanes_of(raw.shape), raw, FAR)
            r.scores[k0 : k0 + count, part * span + q0 : (part + 1) * span] = raw
            top = jnp.max(raw, axis=0, keepdims=True)
            tops.append(jnp.concatenate([jnp.full((1, q0), FAR, F32), top], axis=1) if q0 else top)
        top = functools.reduce(jnp.maximum, tops)
        sums = []
        for part, k0, count, q0 in tiles:
            place = slice(k0, k0 + count), slice(part * span + q0, (part + 1) * span)
            raised = jnp.exp2(r.scores[place] - top[:, q0:]).astype(BF16)
            r.wfc[place] = raised
            sums.append(spread(mm(r.vxt[part, :, k0 : k0 + count], raised), q0))
        att = functools.reduce(jnp.add, sums)
        inverse = 1.0 / att[HEAD : HEAD + 1, :]
        attended = att[:HEAD, :] * inverse
        r.attt[rows, :] = attended.astype(BF16)
        grad_att = r.dot[rows, :].astype(F32)
        delta = jnp.sum(grad_att * attended, axis=0, keepdims=True) * -inverse
        delta_high = delta.astype(BF16).astype(F32)
        row = rows_of((HEAD, span))
        extra = jnp.where(row == 0, delta_high, jnp.where(row == 1, delta - delta_high, 0.0))
        grad_att = jnp.concatenate([grad_att * inverse, extra], axis=0)
        r.ga[...] = grad_att.astype(BF16)
        r.gat[...] = grad_att.T.astype(BF16)

    def attend_back(slot, borrowed, last):
        rows = pl.ds(pl.multiple_of(slot * HEAD, HEAD), HEAD)
        tiles = tiles_of(last)
        sums = []
        for part, k0, count, q0 in tiles:
            keys = slice(k0, k0 + count)
            grad_probs = mm(r.vx[part, keys], r.ga[:, q0:])
            raised = r.wfc[keys, part * span + q0 : (part + 1) * span]
            grad_scores = (raised.astype(F32) * grad_probs).astype(BF16)
            r.dv[part, keys] += mm(raised, r.gat[q0:])
            r.dk[part, keys] += mm(grad_scores, r.q[slot, q0:])
            sums.append(spread(mm(r.kxt[part, :, keys], grad_scores), q0))
        grad_query = functools.reduce(jnp.add, sums)[:HEAD] * (1.0 / math.sqrt(HEAD))
        r.gqt[rows, :] = rotate_back(r, grad_query, borrowed).astype(BF16)

    n_borrowed = jnp.where(mine == 0, 2, 0)
    n_own = jnp.where(mine == parts - 1, heads - 2, heads)
    whole = 2 * (n_borrowed * (partner + 1) + n_own * (mine + 1))

    def half_task(i, done):
        t, backward = i // 2, lax.rem(i, 2) == 1
        borrowed = t < n_borrowed
        own = t - n_borrowed + 4
        own = jnp.where(own >= n_own, own - n_own, own)
        slot = jnp.where(borrowed, heads + t, own)
        last = jnp.where(borrowed, partner, mine)
        for part in range(parts):

            @pl.when((last == part) & ~backward)
            def _():
                attend(slot, part)

            @pl.when((last == part) & backward)
            def _():
                attend_back(slot, jnp.where(borrowed, 1, 0), part)


        @pl.when((mine == 0) & backward & (slot == heads + 1))
        def _():
            for copy in back_copies(r, mine, batch, parts):
                copy.start()

        after = done + last + 1
        before_80, after_80 = done * 80 // whole, after * 80 // whole
        for when, steps in SCHEDULE.items():

            @pl.when((before_80 < when) & (when <= after_80))
            def _():
                step(steps)

        return after

    lax.fori_loop(0, 2 * (n_borrowed + n_own), half_task, 0)
    step(LATE_SCHEDULE[0])

    def packed(part):
        return jnp.where(low, r.dk[part] * (1.0 / LOG2E), pltpu.roll(r.dv[part], HEAD, 1))

    for distance in range(1, parts):
        target = lax.rem(mine - distance + parts, parts)

        @pl.when(target <= high)
        def _():
            r.dkv_out[distance] = packed(target).astype(BF16)
            dkv_copy(r, mine, batch, parts, distance).start()

    if not inside:
        make_early()
    grad_w = mm(r.attt[:width, :], r.cot[...])
    grad_q = mm(r.fit[...], r.gqt[:BLOCK, :], 1, 1)
    for b in range(8):
        core, z = b % 2, b // 2
        for i, name in enumerate(("ua", "ub")):
            rows = slice(b * PIECE + i * PIECE // 2, b * PIECE + (i + 1) * PIECE // 2)
            for q in range(4):
                piece = grad_w[rows, q * BLOCK : (q + 1) * BLOCK] if q < 3 else grad_q[rows]
                keep(name, core, q // 2, q % 2, z, piece)
    step(LATE_SCHEDULE[1])

    r.total[...] = packed(mine)
    for distance in range(1, parts):
        source = lax.rem(mine + distance, parts)

        @pl.when(mine <= jnp.maximum(source, parts - 1 - source))
        def _():
            dkv_copy(r, mine, batch, parts, distance).wait_recv()
            r.total[...] += r.dkv_in[distance].astype(F32)

    pair = r.total[...].T
    r.gkvt[:HEAD, :] = rotate_back(r, pair[:HEAD], 0).astype(BF16)
    r.gkvt[HEAD:, :] = pair[HEAD:].astype(BF16)

    grad_kv = mm(r.fit[...], r.gkvt[...], 1, 1)
    for b in range(8):
        halves = [grad_kv[b * PIECE + i * PIECE // 2 : b * PIECE + (i + 1) * PIECE // 2] for i in range(2)]
        keep("k", b % 2, 0, 0, b // 2, jnp.concatenate(halves, axis=1))
    step(LATE_SCHEDULE[2])
    for i in range(width // LANES):
        columns = slice(i * LANES, (i + 1) * LANES)
        r.act[:, columns] = flip(r.gqt[columns, :]).astype(BF16)
    r.gh[:, :LANES] = flip(r.gkvt[...]).astype(BF16)

    first = mm(r.act[...], r.wq[:, :width], 1, 1) + mm(r.gh[:, :LANES], r.wq[:, width:], 1, 1)
    for i in range(width // LANES):
        (r.dk if i < parts else r.dv)[i % parts] = first[:, i * LANES : (i + 1) * LANES]
    sums = [jnp.zeros((1, width), F32) for _ in range(4)]
    for i in range(span // LANES):
        rows = pl.ds(i * LANES, LANES)
        normed, inverse_std = norm_tile(i)
        first = [(r.dk if j < parts else r.dv)[j % parts, rows, :] for j in range(width // LANES)]
        first, second = jnp.concatenate(first, axis=1), r.second[rows, :]
        for j, term in enumerate((normed * first, first, normed * second, second)):
            sums[j] = sums[j] + jnp.sum(term, axis=0, keepdims=True)
        scaled = first * r.g1[...][None] + second * r.g2[...][None]
        mean_one = jnp.mean(scaled, axis=-1, keepdims=True)
        mean_two = jnp.mean(scaled * normed, axis=-1, keepdims=True)
        back = inverse_std * (scaled - mean_one - normed * mean_two)
        r.si[rows, :] = (r.cot[rows, :].astype(F32) + back).astype(BF16)

    sum_qkv = jnp.concatenate([mm(ones_rows, r.gqt[:width, :], 1, 1), mm(ones_rows, r.gkvt[...], 1, 1)], axis=1)[0:1]
    sum_proj = mm(ones_rows, r.cot[...])[0:1]
    for b in range(8):
        lines = [cut(sum_qkv, b * 112, 112)]
        lines += [r.sum_fc[0:1, b * 384 + i * LANES : b * 384 + (i + 1) * LANES] for i in range(3)]
        lines += [cut(line, b * 96, 96) for line in (sum_proj, *sums)]
        lines.append(jnp.zeros((16 - len(lines), LANES), F32))
        lines = jnp.concatenate(lines, axis=0)
        keep("v", b % 2, 0, 0, b // 2, jnp.concatenate([lines, jnp.zeros_like(lines)], axis=1))
    step(LATE_SCHEDULE[3])
    copies = [pltpu.make_async_copy(r.si, r.input_grads, r.load_sem.at[0])]
    copies[0].start()

    for i in range(width // LANES):
        columns = slice(i * LANES, (i + 1) * LANES)
        r.fi[:, columns] = flip(r.attt[columns, :]).astype(BF16)
    r.x[...] = (r.result[...] + r.x[...].astype(F32) + r.bp[...][None] + mm(r.fi[...], r.wo[...])).astype(BF16)
    copies.append(pltpu.make_async_copy(r.x, r.outputs, r.load_sem.at[1]))
    copies[1].start()

    if inside:
        step(LATE_SCHEDULE[4])
        summing.close()
    else:
        copies.append(pltpu.make_async_copy(r.grads, r.grads_out, r.load_sem.at[2]))
        copies.append(pltpu.make_async_copy(r.wp.at[:, : 2 * BLOCK], r.late_out, r.load_sem.at[3]))
        for copy in copies[2:]:
            copy.start()
    for copy in copies:
        copy.wait()
    for distance in range(1, parts):
        kv_copy(r, mine, batch, parts, distance).wait_send()
        target = lax.rem(mine - distance + parts, parts)

        @pl.when(target <= high)
        def _():
            dkv_copy(r, mine, batch, parts, distance).wait_send()


    @pl.when(mine == parts - 1)
    def _():
        for copy in lent_copies(r, mine, batch, parts):
            copy.wait_send()

    @pl.when(mine == 0)
    def _():
        for copy in back_copies(r, mine, batch, parts):
            copy.wait_send()


def cut(line, start, size):
    line = jnp.concatenate([line, jnp.zeros((1, LANES), F32)], axis=1)
    base = start // LANES * LANES
    line = line[:, base : base + 2 * LANES]
    shift = start - base
    if shift:
        line = pltpu.roll(line, 2 * LANES - shift, 1)
    return jnp.where(lanes_of((1, LANES)) < size, line[:, :LANES], 0.0)


def rotate_back(r, grads, which):
    half = ROT // 2
    one, two = grads[:half], grads[half:ROT]
    cosine, sine = r.cos[which], r.sin[which]
    return jnp.concatenate([one * cosine + two * sine, two * cosine - one * sine, grads[ROT:]], axis=0)


def remote(src, dst, send_sem, recv_sem, peer):
    return pltpu.make_async_remote_copy(
        src_ref=src, dst_ref=dst, send_sem=send_sem, recv_sem=recv_sem, device_id=peer, device_id_type=MESH
    )


def lent_copies(r, mine, batch, parts):
    peer, rows, there = (parts - 1 - mine, batch), LENT * LANES, r.dot.shape[0] - LANES
    return [
        remote(r.lent, r.lent_in, r.lent_sem.at[0, 0], r.lent_sem.at[1, 0], peer),
        remote(
            r.dot.at[rows : rows + LANES],
            r.dot.at[there : there + LANES],
            r.lent_sem.at[0, 1],
            r.lent_sem.at[1, 1],
            peer,
        ),
    ]


def back_copies(r, mine, batch, parts):
    peer, rows, here = (parts - 1 - mine, batch), LENT * LANES, r.dot.shape[0] - LANES
    return [
        remote(ref.at[here : here + LANES], ref.at[rows : rows + LANES], r.back_sem.at[0, j], r.back_sem.at[1, j], peer)
        for j, ref in enumerate((r.attt, r.gqt))
    ]


class Summing:
    def __init__(self, r, mine, batch, parts):
        self.r, self.mine, self.batch, self.parts = r, mine, batch, parts
        y, x = mine // 2, lax.rem(mine, 2)
        self.z, self.core = batch // 2, lax.rem(batch, 2)
        self.axes = {"x": (x, (y * 2 + 1 - x, batch)), "y": (y, ((1 - y) * 2 + x, batch))}
        self.core_peer = (mine, self.z * 2 + 1 - self.core)
        self.z_peers = [(mine, lax.rem(self.z + i, 4) * 2 + self.core) for i in (1, 2, 3)]
        self.seq_peers = [(lax.rem(mine + i, parts), batch) for i in range(1, parts)]
        self.out_copies, self.sent = [], []

    def of(self, _):
        (y, y_peer), (x, x_peer) = self.axes["y"], self.axes["x"]
        p, s = jnp.where(self.core == 0, x, y), jnp.where(self.core == 0, y, x)
        part_x, part_y = x_peer[0], y_peer[0]
        first, then = jnp.where(self.core == 0, part_x, part_y), jnp.where(self.core == 0, part_y, part_x)
        return p, (first, self.batch), s, (then, self.batch)

    def copy(self, name, src, peer, to=None, sem=None):
        start, rows, index = INBOX[name]
        to = start if to is None else to
        return remote(
            src,
            self.r.inbox.at[pl.ds(to, rows)],
            self.r.sum_sem.at[0, index],
            self.r.sum_sem.at[1, index if sem is None else sem],
            peer,
        )

    def start(self, make, *args):
        make(*args).start()
        self.sent.append((make, *args))

    def rows(self, chunk, start, pieces):
        return chunk.ref(self.r).at[pl.ds(pl.multiple_of(start, 16), pieces * chunk.height)]

    def add(self, chunk, start, name, offset, pieces):
        ref, height, from_row = chunk.ref(self.r), chunk.height, INBOX[name][0] + offset

        def one(i, _):
            to = pl.ds(pl.multiple_of(start + i * height, 16), height)
            ref[to, :] += self.r.inbox[pl.ds(pl.multiple_of(from_row + i * height, 16), height), :]
            return 0

        lax.fori_loop(0, pieces, one, 0)

    def pair(self, chunk):
        rows = chunk.rows // 2
        src = chunk.ref(self.r).at[pl.ds(pl.multiple_of(chunk.base + (1 - self.core) * rows, 16), rows)]
        return self.copy("pair " + chunk.name, src, self.core_peer)

    def half(self, chunk):
        p, peer, _, _ = self.of(chunk)
        if chunk.kind == "line":
            return self.copy("half " + chunk.name, self.rows(chunk, chunk.place(self.core, 1 - p, 0, self.z), 2), peer)
        src = self.rows(chunk, chunk.place(self.core, 1 - p, 0, 0), 2 * chunk.count)
        return self.copy("half " + chunk.name, src, peer)

    def quarter(self, chunk):
        p, _, s, peer = self.of(chunk)
        if chunk.kind == "line":
            src = self.rows(chunk, chunk.place(self.core, p, 1 - s, self.z), 1)
        else:
            src = self.rows(chunk, chunk.place(self.core, p, 1 - s, 0), chunk.count)
        return self.copy("quarter " + chunk.name, src, peer)

    def mine_of(self, chunk, z):
        p, _, s, _ = self.of(chunk)
        if chunk.kind in ("line", "whole"):
            return chunk.place(self.core, 0, 0, z)
        return chunk.place(self.core, p, s, 0 if chunk.kind == "plane" else z)

    def pieces(self, chunk):
        return {"plane": chunk.count, "line": 4}.get(chunk.kind, 1)

    def line(self, chunk, i):
        z = lax.rem(self.z + i, 4)
        src = self.rows(chunk, self.mine_of(chunk, z), self.pieces(chunk))
        return self.copy(f"line{i} " + chunk.name, src, self.z_peers[i - 1])

    def plane_line(self, chunk):
        z = int(chunk.name[1:])
        i = lax.rem(z - self.z + 4, 4)
        start, rows, index = INBOX["line1 p"]
        src = self.rows(chunk, self.mine_of(chunk, z), chunk.count)
        return remote(
            src,
            self.r.inbox.at[pl.ds(pl.multiple_of(start + (i - 1) * rows, 16), rows)],
            self.r.sum_sem.at[0, INBOX["line " + chunk.name][2]],
            self.r.sum_sem.at[1, index + i - 1],
            (self.mine, z * 2 + self.core),
        )

    def near(self, name):
        own, rows, _ = INBOX["share0 " + name]
        start, _, index = INBOX["share1 " + name]
        sem = self.r.sum_sem
        return remote(
            self.r.inbox.at[pl.ds(own, rows)],
            self.r.inbox.at[pl.ds(start, rows)],
            sem.at[0, index],
            sem.at[1, index],
            self.of(None)[1],
        )

    def far(self, name):
        own, rows, _ = INBOX["share0 " + name]
        start, _, index = INBOX["share2 " + name]
        sem = self.r.sum_sem
        return remote(
            self.r.inbox.at[pl.ds(own, 2 * rows)],
            self.r.inbox.at[pl.ds(start, 2 * rows)],
            sem.at[0, index],
            sem.at[1, index],
            self.of(None)[3],
        )

    def share(self, name, i):
        start, rows, index = INBOX[f"share{i} " + name]
        own = INBOX["share0 " + name][0]
        return remote(
            self.r.inbox.at[pl.ds(own, rows)],
            self.r.inbox.at[pl.ds(start, rows)],
            self.r.sum_sem.at[0, index],
            self.r.sum_sem.at[1, index],
            self.seq_peers[i - 1],
        )

    def send(self, chunk):
        order = list(CHUNKS).index(chunk.name)
        if order >= SLOTS:
            pl.semaphore_wait(self.r.free_sem.at[order % SLOTS], 1)
        self.start(self.pair, chunk)

    def a(self, chunk):
        self.pair(chunk).wait_recv()
        name, base, p = "pair " + chunk.name, self.core * (chunk.rows // 2), self.of(chunk)[0]
        if chunk.kind in ("line", "whole"):
            pieces = self.pieces(chunk)
            for i in (1, 2, 3, 0):
                start = self.mine_of(chunk, lax.rem(self.z + i, 4))
                self.add(chunk, start, name, start - chunk.base - base, pieces)
                if i:
                    self.start(self.line, chunk, i)
        else:
            for side in (1 - p, p):
                start = chunk.place(self.core, side, 0, 0)
                self.add(chunk, start, name, start - chunk.base - base, 2 * chunk.count)
                if side is not p:
                    self.start(self.half, chunk)
        order = list(CHUNKS).index(chunk.name)
        if order + SLOTS < len(CHUNKS):
            free = self.r.free_sem.at[order % SLOTS]
            pl.semaphore_signal(free, inc=1, device_id=self.core_peer, device_id_type=MESH)

    def total(self, chunk, name, start, pieces):
        rows = pieces * chunk.height
        total = chunk.ref(self.r)[pl.ds(pl.multiple_of(start, 16), rows), :].astype(F32)
        for i in (1, 2, 3):
            at = INBOX[f"line{i} " + name][0]
            total = total + self.r.inbox[at : at + rows, :].astype(F32)
        return total.astype(BF16)

    def give(self, name, value):
        own, rows, _ = INBOX["share0 " + name]
        self.r.inbox[own : own + rows, :] = value
        if name in TWO_STEPS:
            self.start(self.near, name)
            return
        for i in (1, 2, 3):
            self.start(self.share, name, i)

    def g(self, chunk):
        name = "p" if chunk.kind == "plane" else chunk.name
        self.near(name).wait_recv()
        self.start(self.far, name)

    def b(self, chunk):
        p, _, s, _ = self.of(chunk)
        if chunk.kind == "line":
            for i in (1, 2, 3):
                self.line(chunk, i).wait_recv()
            start = self.mine_of(chunk, self.z)
            self.rows(chunk, start, 4)[...] = self.total(chunk, chunk.name, start, 4)
            self.start(self.half, chunk)
            return
        self.half(chunk).wait_recv()
        for side in (1 - s, s):
            offset = side * chunk.count * chunk.height
            self.add(chunk, chunk.place(self.core, p, side, 0), "half " + chunk.name, offset, chunk.count)
            if side is not s:
                self.start(self.quarter, chunk)

    def c(self, chunk):
        p, _, s, _ = self.of(chunk)
        if chunk.kind == "line":
            self.half(chunk).wait_recv()
            for side in (1 - s, s):
                self.add(chunk, chunk.place(self.core, p, side, self.z), "half " + chunk.name, side * chunk.height, 1)
                if side is not s:
                    self.start(self.quarter, chunk)
            return
        self.quarter(chunk).wait_recv()
        name = "quarter " + chunk.name
        if chunk.kind == "plane":
            self.add(chunk, chunk.place(self.core, p, s, 0), name, 0, chunk.count)


            @pl.when(self.z != int(chunk.name[1:]))
            def _():
                self.plane_line(chunk).start()

            return
        for i in (1, 2, 3, 0):
            z = lax.rem(self.z + i, 4)
            self.add(chunk, chunk.place(self.core, p, s, z), name, z * chunk.height, 1)
            if i:
                self.start(self.line, chunk, i)

    def d(self, chunk):
        if chunk.kind == "line":
            p, _, s, _ = self.of(chunk)
            self.quarter(chunk).wait_recv()
            start = chunk.place(self.core, p, s, self.z)
            arrived = INBOX["quarter " + chunk.name][0]
            own = chunk.ref(self.r)[pl.ds(pl.multiple_of(start, 16), PIECE), :]
            self.give(chunk.name, own + self.r.inbox[arrived : arrived + PIECE, :])
            return
        for i in (1, 2, 3):
            self.line(chunk, i).wait_recv()
        self.give(chunk.name, self.total(chunk, chunk.name, self.mine_of(chunk, self.z), 1))

    def d_planes(self, _):
        r, (start, rows, index) = self.r, INBOX["line1 p"]
        p, _, s, _ = self.of(None)
        total = jnp.zeros((rows, BLOCK), F32)
        for z in range(4):
            here = pl.multiple_of(CHUNKS[f"p{z}"].place(self.core, p, s, 0), 16)
            total = jnp.where(self.z == z, r.grads[pl.ds(here, rows), :].astype(F32), total)
        for i in (1, 2, 3):
            at = start + (i - 1) * rows
            arrived = r.inbox.at[at : at + rows]
            remote(arrived, arrived, r.sum_sem.at[0, index], r.sum_sem.at[1, index + i - 1], self.z_peers[3 - i]).wait_recv()
            total = total + arrived[...].astype(F32)
        self.give("p", total.astype(BF16))

    def quarters(self, name):
        refs = [self.r.inbox.at[pl.ds(*INBOX[f"share{i} " + name][:2])] for i in range(4)]
        if name in TWO_STEPS:
            self.far(name).wait_recv()
            _, first, _, then = self.of(None)
            return zip((self.mine, first[0], then[0], 3 - self.mine), refs)
        for i in (1, 2, 3):
            self.share(name, i).wait_recv()
        return zip([lax.rem(self.mine + 4 - i, 4) for i in range(4)], refs)

    def e(self, chunk):
        r, name = self.r, chunk.name
        plane = chunk.kind == "plane"
        arrived = self.quarters("p" if plane else name)
        if chunk.kind == "whole":
            total = functools.reduce(jnp.add, [ref[...].astype(F32) for _, ref in arrived])
            if name == "k":
                for i in range(2):
                    rows = slice(384 + i * PIECE // 2, 384 + (i + 1) * PIECE // 2)
                    r.scores[rows, 768 : 768 + LANES] = total[:, i * LANES : (i + 1) * LANES]
                self.write(r.scores.at[384 : 384 + PIECE, : r.grad_qkv.shape[1]], r.grad_qkv)
                return
            r.grad_bq[...] = total[0, : r.grad_bq.shape[0]]
            for i in range(3):
                r.grad_bfc[i * LANES : (i + 1) * LANES] = total[1 + i, :LANES]
            for i, out in enumerate((r.grad_bp, r.grad_g1, r.grad_s1, r.grad_g2, r.grad_s2)):
                out[...] = total[4 + i, : out.shape[0]]
            return
        for part, ref in arrived:
            y, x = part // 2, lax.rem(part, 2)
            value = ref[...].astype(F32)
            if plane:
                for i in range(3):
                    to = pl.ds(pl.multiple_of(part * PIECE, PIECE), PIECE)
                    r.scores[to, i * BLOCK : (i + 1) * BLOCK] = value[i * PIECE : (i + 1) * PIECE]
            elif name in ("f0", "f1", "f2"):
                top = int(name[1]) * PIECE
                columns = pl.ds(pl.multiple_of(768 + part * BLOCK, BLOCK), BLOCK)
                r.scores[top : top + PIECE, columns] = value
            elif name == "uc":
                rows = pl.ds(pl.multiple_of(384 + y * PIECE // 2, 16), PIECE // 2)
                r.scores[rows, pl.ds(pl.multiple_of((1 + x) * BLOCK, BLOCK), BLOCK)] = value
            else:
                low = name == "ub"
                top = jnp.where(part == 3, 384, 288) + low * PIECE // 2
                left = jnp.where(part == 3, 0, 768 + part * BLOCK)
                rows = pl.ds(pl.multiple_of(top, 16), PIECE // 2)
                r.scores[rows, pl.ds(pl.multiple_of(left, BLOCK), BLOCK)] = value
        if plane:
            self.write(r.scores.at[:384, :768], r.grad_proj)
        elif name in ("f0", "f1", "f2"):
            k = int(name[1])
            src = r.scores.at[k * PIECE : (k + 1) * PIECE, 768 : 768 + 4 * BLOCK]
            self.write(src, r.grad_fc.at[:, 4 * k * BLOCK : 4 * (k + 1) * BLOCK])
        elif name == "ub":
            self.write(r.scores.at[288 : 288 + PIECE, 768 : 768 + 768], r.grad_o)

    def write(self, src, dst):
        copy = pltpu.make_async_copy(src, dst, self.r.out_sem.at[len(self.out_copies)])
        copy.start()
        self.out_copies.append(copy)

    def close(self):
        for copy in self.out_copies:
            copy.wait()
        for make, *args in self.sent:
            make(*args).wait_send()
        for z in range(4):

            @pl.when(self.z != z)
            def _():
                self.plane_line(CHUNKS[f"p{z}"]).wait_send()


TWO_STEPS = ("p", "f0", "f1", "f2")


def make_inbox():
    inbox, rows = {}, SLOTS * 16 * PIECE

    def add(name, count, start=None):
        nonlocal rows
        if start is None:
            start = rows
            rows += count
        inbox[name] = (start, count, len(inbox))

    for order, chunk in enumerate(CHUNKS.values()):
        name, piece = chunk.name, chunk.height
        add("pair " + name, chunk.rows // 2, order % SLOTS * 16 * PIECE)
        if chunk.kind == "plane":
            add("half " + name, 2 * chunk.count * piece)
            add("quarter " + name, chunk.count * piece)
            add("line " + name, chunk.count * piece, 0)
            continue
        if chunk.kind != "whole":
            count = 1 if chunk.kind == "line" else 4
            add("half " + name, 2 * count * piece)
            add("quarter " + name, count * piece)
        for i in (1, 2, 3):
            add(f"line{i} " + name, (4 if chunk.kind == "line" else 1) * piece)
        for i in range(4):
            add(f"share{i} " + name, piece)
    for i in (1, 2, 3):
        add(f"line{i} p", 3 * PIECE)
    for i in range(4):
        add(f"share{i} p", 3 * PIECE)
    return inbox, rows


INBOX, INBOX_ROWS = make_inbox()


def kv_copy(r, source, batch, parts, distance):
    peer = (lax.rem(source + distance, parts), batch)
    return remote(r.kv.at[source], r.kv.at[source], r.kv_sem.at[0, distance], r.kv_sem.at[1, distance], peer)


def dkv_copy(r, mine, batch, parts, distance):
    peer = (lax.rem(mine - distance + parts, parts), batch)
    return remote(
        r.dkv_out.at[distance], r.dkv_in.at[distance], r.dkv_sem.at[0, distance], r.dkv_sem.at[1, distance], peer
    )


def hand_out_kernel(count, *refs):
    sources, targets, held, sem = refs[:count], refs[count : 2 * count], refs[2 * count : -1], refs[-1]
    large = [i for i in range(count) if sources[i].ndim > 1]
    copies = [
        (
            pltpu.make_async_copy(sources[i], held[j], sem.at[0, j]),
            pltpu.make_async_copy(held[j], targets[i], sem.at[1, j]),
        )
        for j, i in enumerate(large)
    ]
    for here, _ in copies:
        here.start()
    for source, target in zip(sources, targets):
        if source.ndim == 1:
            target[...] = source[...]
    for here, there in copies:
        here.wait()
        there.start()
    for _, there in copies:
        there.wait()


def hand_out(results, specs):
    large = [pltpu.VMEM(item.shape, item.dtype) for item in results if item.ndim > 1]
    return pl.pallas_call(
        functools.partial(hand_out_kernel, len(results)),
        out_shape=[jax.ShapeDtypeStruct(item.shape, item.dtype) for item in results],
        in_specs=specs,
        out_specs=specs,
        scratch_shapes=[*large, pltpu.SemaphoreType.DMA((2, len(large)))],
        name="hand_out",
    )(*results)


def per_device(inputs, doc_ids, w_qkv, b_qkv, w_o, w_fc, b_fc, w_proj, b_proj, gain_one, shift_one, gain_two, shift_two, cotangent):
    rows_here, span, width = inputs.shape
    assert rows_here == 1
    parts = lax.axis_size("seq")
    heads = width // HEAD
    hidden_units = w_fc.shape[1]
    merged = width + 2 * HEAD
    inside = parts == 4 and lax.axis_size("batch") == 8
    vmem = pl.BlockSpec(memory_space=pltpu.VMEM)
    anywhere = pl.BlockSpec(memory_space=pl.ANY)

    small = dict(docs=doc_ids, bq=b_qkv, bfc=b_fc, bp=b_proj, g1=gain_one, s1=shift_one, g2=gain_two, s2=shift_two)
    large = dict(x_h=inputs[0], cot_h=cotangent[0], wq_h=w_qkv, wo_h=w_o, wfc_h=w_fc, wp_h=w_proj)
    outs = dict(outputs=((span, width), BF16, anywhere), input_grads=((span, width), BF16, anywhere))
    if inside:
        outs |= dict(
            grad_qkv=((width // 8, merged), F32, anywhere),
            grad_bq=((merged // 8,), F32, vmem),
            grad_o=((width // 8, width), F32, anywhere),
            grad_fc=((width // 8, hidden_units), F32, anywhere),
            grad_bfc=((hidden_units // 8,), F32, vmem),
            grad_proj=((hidden_units // 8, width), F32, anywhere),
            grad_bp=((width // 8,), F32, vmem),
            grad_g1=((width // 8,), F32, vmem),
            grad_s1=((width // 8,), F32, vmem),
            grad_g2=((width // 8,), F32, vmem),
            grad_s2=((width // 8,), F32, vmem),
        )
    else:
        outs |= dict(grads_out=((GRAD_ROWS, BLOCK), BF16, anywhere), late_out=((hidden_units, 2 * BLOCK), BF16, anywhere))
    scratch = dict(
        x=pltpu.VMEM((span, width), BF16),
        cot=pltpu.VMEM((span, width), BF16),
        wq=pltpu.VMEM((width, merged), BF16),
        wo=pltpu.VMEM((width, width), BF16),
        wfc=pltpu.VMEM((width, hidden_units), BF16),
        wp=pltpu.VMEM((hidden_units, width), BF16),
        fi=pltpu.VMEM((span, width), BF16),
        si=pltpu.VMEM((span, width), BF16),
        fit=pltpu.VMEM((width, span), BF16),
        sit=pltpu.VMEM((width, span), BF16),
        cos=pltpu.VMEM((2, ROT // 2, span), F32),
        sin=pltpu.VMEM((2, ROT // 2, span), F32),
        kv=pltpu.VMEM((parts, span, LANES), BF16),
        q=pltpu.VMEM((heads + 2, span, LANES), BF16),
        qt=pltpu.VMEM((heads + 2, LANES, span), BF16),
        lent=pltpu.VMEM((span, LANES), BF16),
        lent_in=pltpu.VMEM((span, LANES), BF16),
        dot=pltpu.VMEM((width + 2 * HEAD, span), BF16),
        act=pltpu.VMEM((span, width), BF16),
        gh=pltpu.VMEM((span, width), BF16),
        result=pltpu.VMEM((span, width), F32),
        second=pltpu.VMEM((span, width), F32),
        sum_fc=pltpu.VMEM((8, hidden_units), F32),
        kx=pltpu.VMEM((parts, span, LANES), BF16),
        kxt=pltpu.VMEM((parts, LANES, span), BF16),
        vx=pltpu.VMEM((parts, span, LANES), BF16),
        vxt=pltpu.VMEM((parts, LANES, span), BF16),
        dk=pltpu.VMEM((parts, span, LANES), F32),
        dv=pltpu.VMEM((parts, span, LANES), F32),
        scores=pltpu.VMEM((span, parts * span), F32),
        ga=pltpu.VMEM((LANES, span), BF16),
        gat=pltpu.VMEM((span, LANES), BF16),
        attt=pltpu.VMEM((width + 2 * HEAD, span), BF16),
        gqt=pltpu.VMEM((width + 2 * HEAD, span), BF16),
        gkvt=pltpu.VMEM((2 * HEAD, span), BF16),
        dkv_out=pltpu.VMEM((parts, span, LANES), BF16),
        dkv_in=pltpu.VMEM((parts, span, LANES), BF16),
        total=pltpu.VMEM((span, LANES), F32),
        grads=pltpu.VMEM((GRAD_ROWS, BLOCK), BF16),
        load_sem=pltpu.SemaphoreType.DMA((6,)),
        kv_sem=pltpu.SemaphoreType.DMA((2, parts)),
        dkv_sem=pltpu.SemaphoreType.DMA((2, parts)),
        lent_sem=pltpu.SemaphoreType.DMA((2, 2)),
        back_sem=pltpu.SemaphoreType.DMA((2, 2)),
    )
    if inside:
        scratch |= dict(
            inbox=pltpu.VMEM((INBOX_ROWS, BLOCK), BF16),
            sum_sem=pltpu.SemaphoreType.DMA((2, len(INBOX))),
            out_sem=pltpu.SemaphoreType.DMA((6,)),
            free_sem=pltpu.SemaphoreType.REGULAR((SLOTS,)),
        )
    names = [*small, *large, *outs, *scratch]
    results = pl.pallas_call(
        functools.partial(layer_kernel, names, parts, inside),
        out_shape=[jax.ShapeDtypeStruct(shape, dtype) for shape, dtype, _ in outs.values()],
        in_specs=[vmem] * len(small) + [anywhere] * len(large),
        out_specs=[spec for _, _, spec in outs.values()],
        scratch_shapes=list(scratch.values()),
        compiler_params=pltpu.CompilerParams(
            collective_id=0, has_side_effects=True, vmem_limit_bytes=63 * 2**20
        ),
        name="layer",
    )(*small.values(), *large.values())
    if inside:
        outputs, input_grads, *shards = hand_out(results, [spec for _, _, spec in outs.values()])
        return (outputs[None], input_grads[None], *shards)
    outputs, input_grads, *shards = results

    grads, late = shards
    planes = [CHUNKS[f"p{z}"].unfold(grads).transpose(0, 1, 2, 4, 3, 5).reshape(-1, width) for z in range(4)]
    proj = jnp.concatenate(planes)
    columns = [
        CHUNKS[name].unfold(grads).transpose(3, 0, 4, 1, 2, 5).reshape(width, 4 * BLOCK) for name in ("f0", "f1", "f2")
    ]
    fc = jnp.concatenate(columns, axis=1)
    halves = [CHUNKS[name].unfold(late[:, :BLOCK]).transpose(3, 0, 4, 1, 2, 5) for name in ("ua", "ub")]
    both = jnp.stack(halves, axis=2).reshape(width, 4 * BLOCK)
    o = both[:, :width]
    rest = CHUNKS["uc"].unfold(late[:, BLOCK:]).transpose(3, 0, 1, 4, 2, 5).reshape(width, 2 * BLOCK)
    last = CHUNKS["k"].unfold(late[:, BLOCK:]).reshape(2, 4, PIECE // 2, 2, LANES).transpose(1, 0, 3, 2, 4)
    qkv = jnp.concatenate([both[:, width:], rest, last.reshape(width, LANES)], axis=1)
    blocks = 8
    lines = CHUNKS["v"].unfold(late[:, BLOCK:]).transpose(1, 0, 2, 3).reshape(blocks, 16, BLOCK)[..., :LANES]
    vectors = [lines[:, 0, : merged // blocks], lines[:, 1:4]] + [lines[:, i, : width // blocks] for i in range(4, 9)]
    vectors = [vector.reshape(-1) for vector in vectors]
    every = [qkv, vectors[0], o, fc, vectors[1], proj, *vectors[2:]]
    shards = [lax.psum_scatter(item, "batch", scatter_dimension=0, tiled=True) for item in every]
    shards = [lax.psum(item, "seq").astype(F32) for item in shards]
    return (outputs[None], input_grads[None], *shards)


def solution(mesh):
    whole, part = P(), P("batch", "seq", None)
    in_specs = (part, P("batch", None), *[whole] * 11, part)
    matrix, vector = P("batch", None), P("batch")
    out_specs = (part, part, matrix, vector, matrix, matrix, vector, matrix, *[vector] * 5)
    return jax.shard_map(per_device, mesh=mesh, in_specs=in_specs, out_specs=out_specs, check_vma=False)
```

profile of v0, /device:TPU:0, one launch (start us, length us, event | category | flops | bytes accessed | tf_op | source)
XLA Modules:
  0.0 116.2 jit_solution(14342920205973254919)
XLA Ops:
  0.7 110.1 %layer.1 = (bf16[512,768]{1,0:T(8,128)(2,1)}, bf16[512,768]{1,0:T(8,128)(2,1)}, f32[96,896]{1,0:T(8,128)}, f32[112]{0:T(128)}, f32[96,768]{1,0:T(8,128)}, /*inde...) custom-call(s32[1,2048]{1,0:T(1,128)} %refs_0_.1, ...), custom_call_target="tpu_custom_call" | custom-call | tf_op jit(solution)/shard_map/layer/pallas_call | solution.py:1113
  110.8 5.2 %hand_out.1 = (bf16[512,768]{1,0:T(8,128)(2,1)}, bf16[512,768]{1,0:T(8,128)(2,1)}, f32[96,896]{1,0:T(8,128)}, f32[112]{0:T(128)}, f32[96,768]{1,0:T(8,128)}, /*i...) custom-call(bf16[512,768]{1,0:T(8,128)(2,1)} %get-tuple-element.39.r, ...), custom_call_target="tpu_custom_call" | custom-call | tf_op jit(solution)/shard_map/hand_out/pallas_call | solution.py:1019
where the time goes:
time: 116 us
  Pallas kernels  115 us (99%)
    pallas_call x1, Pallas kernels, per_device(): pl.pallas_call(functools.partial(layer_kernel, names, parts, inside), out...  110 us
    pallas_call x1, Pallas kernels, hand_out(): pl.pallas_call(functools.partial(hand_out_kernel, len(results)), out_shap...  5.25 us

commit v1 on v0

--- a/solution.py
+++ b/solution.py
@@ -69,7 +69,7 @@
         ("p1", "plane", PIECE, 3, None),
         ("f0", "line", PIECE, 4, None),
         ("p2", "plane", PIECE, 3, None),
-        ("f1", "block", PIECE, 4, None),
+        ("f1", "line", PIECE, 4, None),
         ("p3", "plane", PIECE, 3, None),
         ("f2", "block", PIECE, 4, None),
         ("uc", "block", PIECE // 2, 4, 1),
@@ -108,36 +108,36 @@
 EARLY_DONE = 64
 
 FEED_SCHEDULE = [
-    ([], ["send:p0"], []),
-    (["a:p0"], [], ["send:p1", "send:f0"]),
-    (["a:f0", "a:p1"], ["send:p2"], ["send:f1"]),
-    (["b:p0"], ["a:f1", "send:p3"], []),
-    [],
+    ([], [], []),
+    ([], ["send:p0", "send:p1"], ["send:f0"]),
+    (["a:f0", "a:p1"], ["a:p0"], ["send:p2"]),
+    ([], [], ["a:p2"]),
+    ["send:f1", "b:p1", "send:p3", "send:f2"],
 ]
 
 SCHEDULE = {
-    4: ["a:p2", "send:f2"],
-    12: ["c:p0", "a:f2"],
-    16: ["b:f1"],
-    20: ["a:p3"],
-    28: ["b:f2"],
-    32: ["c:f1"],
-    36: ["b:f0", "b:p2"],
-    44: ["c:f2", "b:p1"],
-    48: ["c:f0"],
-    60: ["b:p3", "d:f1"],
-    EARLY_DONE: ["make:uc", "d:f2", "send:uc", "c:p1"],
-    68: ["c:p2", "a:uc"],
-    72: ["g:f2", "c:p3", "g:f1"],
-    76: ["b:uc", "d:f0"],
+    4: ["a:p3"],
+    8: ["a:f2"],
+    12: ["a:f1", "b:p2"],
+    28: ["c:p1"],
+    32: ["b:f0"],
+    36: ["b:f2", "b:p0"],
+    44: ["c:f0"],
+    48: ["c:f2"],
+    52: ["c:p0"],
+    60: ["b:p3"],
+    EARLY_DONE: ["make:uc", "send:uc", "d:f0"],
+    68: ["a:uc", "c:p3"],
+    72: ["b:f1", "g:f0"],
+    76: ["b:uc"],
 }
 
 LATE_SCHEDULE = [
-    [],
-    ["send:ua", "c:uc", "e:f1", "a:ua", "e:f2", "send:ub", "a:ub"],
-    ["send:k", "b:ua", "g:f0", "a:k"],
-    ["b:ub", "send:v", "d_planes:p0", "c:ua", "d:uc", "a:v", "c:ub", "d:k", "e:f0", "g:p0", "d:ua", "d:v", "d:ub"],
-    ["e:uc", "e:v", "e:ua", "e:p0", "e:ub", "e:k"],
+    ["c:f1"],
+    ["c:p2", "c:uc", "send:ua", "a:ua", "send:ub", "d:f2", "a:ub"],
+    ["send:k", "b:ua", "a:k", "b:ub", "d:f1", "c:ua", "d_planes:p0", "g:f2"],
+    ["g:f1", "c:ub", "send:v", "d:uc", "g:p0", "a:v", "d:k"],
+    ["d:ua", "e:f0", "e:f1", "e:f2", "d:ub", "d:v", "e:p0", "e:ua", "e:uc", "e:ub", "e:k", "e:v"],
 ]
 
 LENT = 5
@@ -246,8 +246,15 @@
     low = lane < HEAD
     key_value = rotate(key_value, jnp.where(low, table_cos, 1.0), jnp.where(low, table_sin, 0.0))
     r.kv[mine] = key_value.astype(BF16)
+
+    def needs(part, source):
+        return (part > source) | (part == 0)
+
     for distance in range(1, parts):
-        kv_copy(r, mine, batch, parts, distance).start()
+
+        @pl.when(needs(lax.rem(mine + distance, parts), mine))
+        def _():
+            kv_copy(r, mine, batch, parts, distance).start()
 
     feature_row = rows_of((LANES, span)) - HEAD
 
@@ -264,7 +271,7 @@
         tile = rotate(tile, table_cos, table_sin) * (LOG2E / math.sqrt(HEAD))
         keep_queries(2 * i, tile, query_feature)
         if i == LENT:
-            r.lent[...] = tile.astype(BF16)
+            r.dkv_out[0] = tile.astype(BF16)
 
     loads[2].wait()
     loads[3].wait()
@@ -293,7 +300,8 @@
                 def _():
                     step(steps[i])
 
-    plane, line, block = CHUNKS["p0"], CHUNKS["f0"], CHUNKS["f1"]
+    plane, line, block = CHUNKS["p0"], CHUNKS["f0"], CHUNKS["f2"]
+    lines = sum(chunk.kind == "line" for chunk in CHUNKS.values())
 
     def feed_forward(g, _):
         columns = pl.ds(pl.multiple_of(g * group, LANES), group)
@@ -319,8 +327,8 @@
             for b in range(8):
                 c, z = b % 2, b // 2
                 p, s = line.split(c, y, x)
-                later = block.place(c, p, s, z) + (chunk - 1) * block.rows
-                to = jnp.where(chunk == 0, line.place(c, p, s, z), later)
+                later = block.place(c, p, s, z) + (chunk - 2) * block.rows
+                to = jnp.where(chunk < lines, line.place(c, p, s, z) + chunk * line.rows, later)
                 piece = grad_w[b * PIECE : (b + 1) * PIECE, k * BLOCK : (k + 1) * BLOCK]
                 r.grads[pl.ds(pl.multiple_of(to, 16), PIECE), :] = piece.astype(BF16)
         feed_steps(g, 2)
@@ -333,8 +341,13 @@
     step(FEED_SCHEDULE[4])
 
     for distance in range(1, parts):
-        kv_copy(r, lax.rem(mine - distance + parts, parts), batch, parts, distance).wait_recv()
-    for part in range(parts):
+        source = lax.rem(mine - distance + parts, parts)
+
+        @pl.when(needs(mine, source))
+        def _():
+            kv_copy(r, source, batch, parts, distance).wait_recv()
+
+    def prepare(part):
         apart = (feature_row >= 0) & (feature_row < 8) & (feature_row != docs_row(part))
         key_feature = jnp.where(apart, FAR, 0.0).T
         pair = r.kv[part].astype(F32)
@@ -345,12 +358,15 @@
         r.vx[part] = values.astype(BF16)
         r.vxt[part] = values.T.astype(BF16)
 
+    for part in range(parts):
+        pl.when((mine >= part) | (mine == 0))(functools.partial(prepare, part))
+
     @pl.when(mine == 0)
     def _():
         for copy in lent_copies(r, mine, batch, parts):
             copy.wait_recv()
         feature = jnp.where(feature_row == docs_row(partner), 1.0, 0.0).T
-        keep_queries(heads, r.lent_in[...].astype(F32), feature)
+        keep_queries(heads, r.dkv_in[0].astype(F32), feature)
 
     r.dk[...] = jnp.zeros_like(r.dk)
     r.dv[...] = jnp.zeros_like(r.dv)
@@ -367,6 +383,13 @@
                 rows = slice(b * PIECE + y * PIECE // 2, b * PIECE + (y + 1) * PIECE // 2)
                 for x in range(2):
                     keep("uc", b % 2, y, x, b // 2, grad_q[rows, x * BLOCK : (x + 1) * BLOCK])
+
+    def packed(part):
+        return jnp.where(low, r.dk[part] * (1.0 / LOG2E), pltpu.roll(r.dv[part], HEAD, 1))
+
+    def send_key_grads(distance):
+        r.dkv_out[distance] = packed(lax.rem(mine - distance + parts, parts)).astype(BF16)
+        dkv_copy(r, mine, batch, parts, distance).start()
 
     mid = span // 2
 
@@ -462,16 +485,11 @@
     lax.fori_loop(0, 2 * (n_borrowed + n_own), half_task, 0)
     step(LATE_SCHEDULE[0])
 
-    def packed(part):
-        return jnp.where(low, r.dk[part] * (1.0 / LOG2E), pltpu.roll(r.dv[part], HEAD, 1))
-
-    for distance in range(1, parts):
-        target = lax.rem(mine - distance + parts, parts)
-
-        @pl.when(target <= high)
+    for distance in reversed(range(1, parts)):
+
+        @pl.when(lax.rem(mine - distance + parts, parts) <= high)
         def _():
-            r.dkv_out[distance] = packed(target).astype(BF16)
-            dkv_copy(r, mine, batch, parts, distance).start()
+            send_key_grads(distance)
 
     if not inside:
         make_early()
@@ -486,16 +504,16 @@
                 keep(name, core, q // 2, q % 2, z, piece)
     step(LATE_SCHEDULE[1])
 
-    r.total[...] = packed(mine)
+    r.dk[mine] = packed(mine)
     for distance in range(1, parts):
         source = lax.rem(mine + distance, parts)
 
         @pl.when(mine <= jnp.maximum(source, parts - 1 - source))
         def _():
             dkv_copy(r, mine, batch, parts, distance).wait_recv()
-            r.total[...] += r.dkv_in[distance].astype(F32)
-
-    pair = r.total[...].T
+            r.dk[mine] += r.dkv_in[distance].astype(F32)
+
+    pair = r.dk[mine].T
     r.gkvt[:HEAD, :] = rotate_back(r, pair[:HEAD], 0).astype(BF16)
     r.gkvt[HEAD:, :] = pair[HEAD:].astype(BF16)
 
@@ -557,7 +575,11 @@
     for copy in copies:
         copy.wait()
     for distance in range(1, parts):
-        kv_copy(r, mine, batch, parts, distance).wait_send()
+
+        @pl.when(needs(lax.rem(mine + distance, parts), mine))
+        def _():
+            kv_copy(r, mine, batch, parts, distance).wait_send()
+
         target = lax.rem(mine - distance + parts, parts)
 
         @pl.when(target <= high)
@@ -602,7 +624,7 @@
 def lent_copies(r, mine, batch, parts):
     peer, rows, there = (parts - 1 - mine, batch), LENT * LANES, r.dot.shape[0] - LANES
     return [
-        remote(r.lent, r.lent_in, r.lent_sem.at[0, 0], r.lent_sem.at[1, 0], peer),
+        remote(r.dkv_out.at[0], r.dkv_in.at[0], r.lent_sem.at[0, 0], r.lent_sem.at[1, 0], peer),
         remote(
             r.dot.at[rows : rows + LANES],
             r.dot.at[there : there + LANES],
@@ -1072,8 +1094,6 @@
         kv=pltpu.VMEM((parts, span, LANES), BF16),
         q=pltpu.VMEM((heads + 2, span, LANES), BF16),
         qt=pltpu.VMEM((heads + 2, LANES, span), BF16),
-        lent=pltpu.VMEM((span, LANES), BF16),
-        lent_in=pltpu.VMEM((span, LANES), BF16),
         dot=pltpu.VMEM((width + 2 * HEAD, span), BF16),
         act=pltpu.VMEM((span, width), BF16),
         gh=pltpu.VMEM((span, width), BF16),
@@ -1094,7 +1114,6 @@
         gkvt=pltpu.VMEM((2 * HEAD, span), BF16),
         dkv_out=pltpu.VMEM((parts, span, LANES), BF16),
         dkv_in=pltpu.VMEM((parts, span, LANES), BF16),
-        total=pltpu.VMEM((span, LANES), F32),
         grads=pltpu.VMEM((GRAD_ROWS, BLOCK), BF16),
         load_sem=pltpu.SemaphoreType.DMA((6,)),
         kv_sem=pltpu.SemaphoreType.DMA((2, parts)),

time: 116 us -> 114 us (0.983)
  Pallas kernels: 115 us -> 113 us
    pallas_call x1, Pallas kernels: 110 us -> 107 us  [per_device(): pl.pallas_call(functools.partial(layer_kernel, names, parts, inside), out...]
where the time goes in v1:
time: 114 us
  Pallas kernels  113 us (99%)
    pallas_call x1, Pallas kernels, per_device(): pl.pallas_call(functools.partial(layer_kernel, names, parts, inside), out...  107 us
    pallas_call x1, Pallas kernels, hand_out(): pl.pallas_call(functools.partial(hand_out_kernel, len(results)), out_shap...  5.25 us

profile of v1, /device:TPU:0, one launch (start us, length us, event | category | flops | bytes accessed | tf_op | source)
XLA Modules:
  0.0 113.5 jit_solution(15129210058118111372)
XLA Ops:
  0.7 107.4 %layer.1 = (bf16[512,768]{1,0:T(8,128)(2,1)}, bf16[512,768]{1,0:T(8,128)(2,1)}, f32[96,896]{1,0:T(8,128)}, f32[112]{0:T(128)}, f32[96,768]{1,0:T(8,128)}, /*inde...) custom-call(s32[1,2048]{1,0:T(1,128)} %refs_0_.1, ...), custom_call_target="tpu_custom_call" | custom-call | tf_op jit(solution)/shard_map/layer/pallas_call | solution.py:1132
  108.1 5.2 %hand_out.1 = (bf16[512,768]{1,0:T(8,128)(2,1)}, bf16[512,768]{1,0:T(8,128)(2,1)}, f32[96,896]{1,0:T(8,128)}, f32[112]{0:T(128)}, f32[96,768]{1,0:T(8,128)}, /*i...) custom-call(bf16[512,768]{1,0:T(8,128)(2,1)} %get-tuple-element.39.r, ...), custom_call_target="tpu_custom_call" | custom-call | tf_op jit(solution)/shard_map/hand_out/pallas_call | solution.py:1041

commit v2 on v1

--- a/solution.py
+++ b/solution.py
@@ -1017,13 +1017,17 @@
 def hand_out_kernel(count, *refs):
     sources, targets, held, sem = refs[:count], refs[count : 2 * count], refs[2 * count : -1], refs[-1]
     large = [i for i in range(count) if sources[i].ndim > 1]
-    copies = [
-        (
-            pltpu.make_async_copy(sources[i], held[j], sem.at[0, j]),
-            pltpu.make_async_copy(held[j], targets[i], sem.at[1, j]),
-        )
-        for j, i in enumerate(large)
-    ]
+    copies = []
+    for j, i in enumerate(large):
+        half = sources[i].shape[0] // 2
+        for k in range(2):
+            rows, at = pl.ds(k * half, half), 2 * j + k
+            copies.append(
+                (
+                    pltpu.make_async_copy(sources[i].at[rows], held[j].at[rows], sem.at[0, at]),
+                    pltpu.make_async_copy(held[j].at[rows], targets[i].at[rows], sem.at[1, at]),
+                )
+            )
     for here, _ in copies:
         here.start()
     for source, target in zip(sources, targets):
@@ -1043,7 +1047,7 @@
         out_shape=[jax.ShapeDtypeStruct(item.shape, item.dtype) for item in results],
         in_specs=specs,
         out_specs=specs,
-        scratch_shapes=[*large, pltpu.SemaphoreType.DMA((2, len(large)))],
+        scratch_shapes=[*large, pltpu.SemaphoreType.DMA((2, 2 * len(large)))],
         name="hand_out",
     )(*results)
 

time: 114 us -> 114 us (level)
  no operation moved by 1% of the time
where the time goes in v2:
time: 114 us
  Pallas kernels  113 us (99%)
    pallas_call x1, Pallas kernels, per_device(): pl.pallas_call(functools.partial(layer_kernel, names, parts, inside), out...  107 us
    pallas_call x1, Pallas kernels, hand_out(): pl.pallas_call(functools.partial(hand_out_kernel, len(results)), out_shap...  5.46 us

profile of v2, /device:TPU:0, one launch (start us, length us, event | category | flops | bytes accessed | tf_op | source)
XLA Modules:
  0.0 113.7 jit_solution(15278411939931815245)
XLA Ops:
  0.7 107.4 %layer.1 = (bf16[512,768]{1,0:T(8,128)(2,1)}, bf16[512,768]{1,0:T(8,128)(2,1)}, f32[96,896]{1,0:T(8,128)}, f32[112]{0:T(128)}, f32[96,768]{1,0:T(8,128)}, /*inde...) custom-call(s32[1,2048]{1,0:T(1,128)} %refs_0_.1, ...), custom_call_target="tpu_custom_call" | custom-call | tf_op jit(solution)/shard_map/layer/pallas_call | solution.py:1136
  108.1 5.5 %hand_out.1 = (bf16[512,768]{1,0:T(8,128)(2,1)}, bf16[512,768]{1,0:T(8,128)(2,1)}, f32[96,896]{1,0:T(8,128)}, f32[112]{0:T(128)}, f32[96,768]{1,0:T(8,128)}, /*i...) custom-call(bf16[512,768]{1,0:T(8,128)(2,1)} %get-tuple-element.39.r, ...), custom_call_target="tpu_custom_call" | custom-call | tf_op jit(solution)/shard_map/hand_out/pallas_call | solution.py:1045
